TPU v7x, 256 devices: a whole 4x4x8 slice. The times are simulated.
256 devices in a mesh: blk: 64 (over x, y_hi, z), rep: 4 (over y_lo, core).
Axes of the slice: x: 4, y: 4 (y_hi: 2, y_lo: 2; y = y_hi * 2 + y_lo), z: 8, core: 2. Of those that a mesh axis runs over, the one named last changes fastest.
Arguments:
- features: bfloat16 [32768, 512], P('blk', 'rep'), may hold values from -6 to 6
- row_target: int32 [32768], P('blk'), may hold values from 0 to 32767, as said below
- tile_values: bfloat16 [64, 64, 4, 128, 128], P('blk'), may hold values from -0.25 to 0.25
- tile_rows: int32 [64, 64, 4], P('blk'), may hold values from 0 to 3, as said below
- tile_cols: int32 [64, 64, 4], P('blk'), may hold values from 0 to 3, as said below
- tile_counts: int32 [64, 64], P('blk'), may hold values from 0 to 4, as said below
- weight: bfloat16 [512, 512], P('rep'), may hold values from -0.25 to 0.25
- layer_bias: float32 [512], replicated, may hold values from -3 to 3
- out_grad: bfloat16 [32768, 512], P('blk'), may hold values from -0.75 to 0.75
Outputs:
- output: bfloat16 [32768, 512], P(('blk', 'rep'))
- weight_grad: float32 [512, 512], P('rep')
- bias_grad: float32 [512], replicated
- feature_grad: bfloat16 [32768, 512], P('blk', 'rep')
Inputs may be any that keep to these rules, and one draw needn't show every extreme that they name: `row_target`: a permutation of the 32768 rows; the rows of one loader block of 512 rows bound for one partition number at most 16, and this many in every draw. `tile_rows`: within one pair of partitions the live slots name distinct tile positions. `tile_cols`: within one pair of partitions the live slots name distinct tile positions. `tile_counts`: every pair of a partition with itself has all 4 slots live; each row partition has live slots with exactly 6 other partitions, and none with the rest.
All inputs are finite; a program needn't handle non-finite values.
Results may differ from a plain program's by a relative error of at most 0.0061.
Values may be sent and summed in bfloat16 or wider, within the bound.
A program may use at most 128 MiB of HBM per device.

v0:
```python
import jax
import jax.numpy as jnp
from jax import lax
from jax.sharding import PartitionSpec as P

PARTNERS = 6
BF = jnp.bfloat16
F32 = jnp.float32


def one_hot(condition):
    return condition.astype(BF)


def dot(a, b, dims=((1,), (0,))):
    return lax.dot_general(a, b, (dims, ((), ())), preferred_element_type=F32)


def exchange(x):
    return lax.all_to_all(x, "blk", split_axis=0, concat_axis=0, tiled=True)


def per_device(
    features,
    row_target,
    tile_values,
    tile_rows,
    tile_cols,
    tile_counts,
    weight,
    layer_bias,
    out_grad,
):
    blocks = lax.axis_size("blk")
    members = lax.axis_size("rep")
    me = lax.axis_index("blk")
    member = lax.axis_index("rep")
    rows, cols = features.shape
    slots, tile = tile_values.shape[2:4]
    tiles = rows // tile
    bucket = 2 * rows // blocks
    piece = rows // blocks
    full_weight = lax.all_gather(weight, "rep", axis=0, tiled=True)
    all_counts = lax.all_gather(tile_counts[0], "blk", axis=0).reshape(blocks, blocks)
    ids = jnp.arange(blocks, dtype=jnp.int32)
    target = row_target // rows
    landing = row_target % rows
    hits = target[None, :] == ids[:, None]
    at = jnp.arange(rows, dtype=jnp.int32)
    earlier = dot(one_hot(hits), one_hot(at[:, None] < at[None, :]))
    rank = jnp.sum(jnp.where(hits, earlier, 0.0), axis=0).astype(jnp.int32)
    slot = target * bucket + rank
    to_slot = slot[None, :] == jnp.arange(blocks * bucket, dtype=jnp.int32)[:, None]
    send_rows = dot(one_hot(to_slot), features).astype(BF)
    send_where = jnp.sum(jnp.where(to_slot, landing[None, :] + 1, 0), axis=1) - 1
    got_rows = exchange(send_rows.reshape(blocks, bucket, cols)).reshape(-1, cols)
    got_where = exchange(send_where.reshape(blocks, bucket)).reshape(-1)
    regrouped = dot(one_hot(got_where[None, :] == at[:, None]), got_rows).astype(BF)
    partner = (all_counts > 0) & (ids[:, None] != ids[None, :])
    order = dot(one_hot(partner), one_hot(ids[:, None] < ids[None, :]))
    wanted = jnp.arange(PARTNERS, dtype=F32)
    choose = partner[:, None, :] & (order[:, None, :] == wanted[None, :, None])
    flat_choose = one_hot(choose).reshape(blocks * PARTNERS, blocks)
    mine = lax.dynamic_index_in_dim(choose, me, 0, keepdims=False)
    mine = jnp.concatenate([mine, (ids == me)[None]], axis=0).astype(jnp.int32)
    which = jnp.sum(mine * ids[None, :], axis=1)
    meets = PARTNERS + 1
    row_of = jnp.sum(mine[:, :, None] * tile_rows[0][None], axis=1)
    col_of = jnp.sum(mine[:, :, None] * tile_cols[0][None], axis=1)
    live = jnp.sum(mine * tile_counts[0][None], axis=1)
    live = jnp.arange(slots, dtype=jnp.int32)[None, :] < live[:, None]
    tile_ids = jnp.arange(tiles, dtype=jnp.int32)
    spot = (
        live[:, :, None, None]
        & (row_of[:, :, None, None] == tile_ids[None, None, :, None])
        & (col_of[:, :, None, None] == tile_ids[None, None, None, :])
    )
    adjacency = []
    for k in range(meets):
        values = lax.dynamic_index_in_dim(tile_values[0], which[k], 0, keepdims=False)
        dense = jnp.zeros((tiles, tile, tiles, tile), BF)
        for s in range(slots):
            dense = jnp.where(spot[k, s][:, None, :, None], values[s][None, :, None, :], dense)
        adjacency.append(dense.reshape(rows, rows))
    adjacency = jnp.concatenate(adjacency, axis=1)
    spread = exchange(regrouped.reshape(blocks, piece, cols)).reshape(blocks, piece * cols)
    served = dot(flat_choose, spread).astype(BF)
    served = exchange(served.reshape(blocks, PARTNERS * piece, cols))
    served = served.reshape(blocks, PARTNERS, piece, cols).transpose(1, 0, 2, 3)
    inputs = jnp.concatenate([served.reshape(PARTNERS * rows, cols), regrouped], axis=0)
    mixed = dot(adjacency, inputs).astype(BF)
    full_mixed = lax.all_gather(mixed, "rep", axis=1, tiled=True)
    pre = dot(full_mixed, full_weight) + layer_bias
    sigma = jax.nn.sigmoid(pre)
    share = rows // members
    output = lax.dynamic_slice_in_dim((pre * sigma).astype(BF), member * share, share, 0)
    pre_grad = (out_grad.astype(F32) * sigma * (1.0 + pre * (1.0 - sigma))).astype(BF)
    mixed_grad = dot(pre_grad, weight, ((1,), (1,))).astype(BF)
    terms = dot(adjacency, mixed_grad, ((0,), (0,)))
    own = terms[PARTNERS * rows :]
    away = terms[: PARTNERS * rows].astype(BF).reshape(PARTNERS, blocks, piece, cols)
    away = exchange(away.transpose(1, 0, 2, 3).reshape(blocks, PARTNERS * piece, cols))
    away = away.reshape(blocks * PARTNERS, piece * cols)
    summed = dot(flat_choose, away, ((0,), (0,)))
    back = exchange(summed.reshape(blocks, piece, cols)).reshape(rows, cols)
    feature_grad = (back + own).astype(BF)
    weight_part = dot(mixed, pre_grad, ((0,), (0,)))
    bias_part = jnp.sum(pre_grad.astype(F32), axis=0)
    bias_grad = jnp.sum(lax.all_gather(bias_part, "blk", axis=0), axis=0)
    wide = weight_part.shape[1]
    weight_part = exchange(weight_part.reshape(blocks, -1, wide))
    weight_grad = lax.all_gather(jnp.sum(weight_part, axis=0), "blk", axis=0, tiled=True)
    return (output, weight_grad, bias_grad, feature_grad)


def solution(mesh):
    in_specs = (
        P("blk", "rep"),
        P("blk"),
        P("blk", None, None, None, None),
        P("blk", None, None),
        P("blk", None, None),
        P("blk", None),
        P("rep", None),
        P(),
        P("blk", None),
    )
    out_specs = (P(("blk", "rep"), None), P("rep", None), P(), P("blk", "rep"))
    return jax.shard_map(
        per_device, mesh=mesh, in_specs=in_specs, out_specs=out_specs, check_vma=False
    )
```

profile of v0, /device:TPU:32, one launch (start us, length us, event | category | flops | bytes accessed | tf_op | source)
XLA Modules:
  0.0 724.9 jit_solution(7916404086749864458)
XLA Ops:
  0.6 0.7 fusion.22
  1.4 0.2 fusion.5
  1.6 0.3 select_reduce_fusion
  1.9 0.7 sub.17
  2.6 14.2 %all-to-all-start = ((s32[64,1,16]{2,1,0:T(1,128)}), s32[64,1,16]{2,1,0:T(1,128)S(1)}, u32[]{:S(2)}, u32[]{:S(2)}) async-start(s32[64,1,16]{2,1,0:T(1,128)} %bitcast.70), calls=%async_computation | async-start | bytes 65536 | tf_op jit(solution)/shard_map/all_to_all | solution.py:20
  16.8 175.0 %all-gather.1 = s32[64,1,64]{2,1,0:T(1,128)S(1)} all-gather(s32[1,1,64]{2,1,0:T(1,128)} %bitcast.215), channel_id=1, replica_groups=mesh['blk'=64,'rep'=4] {'blk'}, dimensions={0}, use_global_device_ids=true | all-gather | bytes 16640 | tf_op jit(solution)/shard_map/all_gather | solution.py:44
  191.9 0.1 fusion.19
  192.1 0.8 select_reduce_fusion.1
  192.9 0.7 fusion.27
  202.6 1.0 multiply_reduce_fusion.1
  203.8 0.6 slice_bitcast_fusion.3
  208.9 2.0 dynamic-slice_bitcast_fusion.3
  210.9 0.4 select_select_fusion.5
  211.4 0.4 select_select_fusion.6
  211.8 0.4 select_select_fusion.4
  212.3 1.2 fusion.2
  213.5 11.2 %all-to-all-start.1 = ((bf16[64,16,128]{2,1,0:T(8,128)(2,1)}), bf16[64,16,128]{2,1,0:T(8,128)(2,1)}, u32[]{:S(2)}, u32[]{:S(2)}) async-start(bf16[64,16,128]{2,1,0:T(8,128)(2,1)} %bitcast.71), calls=%async_computation.1 | async-start | bytes 524288 | tf_op jit(solution)/shard_map/all_to_all | solution.py:20
  224.6 0.4 select_select_fusion.3
  225.1 0.4 select_select_fusion.2
  225.5 1.3 select_select_fusion.1
  226.8 0.5 broadcast.245
  227.3 1.5 reduce.4
  228.9 9.0 %all-to-all-done.1 = bf16[64,16,128]{2,1,0:T(8,128)(2,1)} async-done(((bf16[64,16,128]{2,1,0:T(8,128)(2,1)}), bf16[64,16,128]{2,1,0:T(8,128)(2,1)}, u32[]{:S(2)}, u32[]{:S(2)}) %all-to-all-start.1) | async-done | bytes 262176 | tf_op jit(solution)/shard_map/all_to_all | solution.py:20
  237.9 2.1 fusion.3
  240.0 5.7 all-to-all-start.2
  245.7 1.2 select_select_fusion
  247.0 0.7 and.71
  247.6 0.9 bitcast_dynamic-update-slice_fusion.6
  248.5 9.1 %all-to-all-done.2 = bf16[64,8,128]{2,1,0:T(8,128)(2,1)} async-done(((bf16[64,8,128]{2,1,0:T(8,128)(2,1)}), bf16[64,8,128]{2,1,0:T(8,128)(2,1)}, u32[]{:S(2)}, u32[]{:S(2)}) %all-to-all-start.2) | async-done | bytes 131104 | tf_op jit(solution)/shard_map/all_to_all | solution.py:20
  257.7 1.3 convolution_convert_fusion
  259.0 1.2 reshape.423
  260.2 5.3 all-to-all-start.3
  265.4 8.0 %all_gather.20 = bf16[512,512]{1,0:T(8,128)(2,1)} all-gather(bf16[128,512]{1,0:T(8,128)(2,1)} %param.15), channel_id=1, replica_groups=mesh['blk'=64,'rep'=4] {'rep'}, dimensions={0}, use_global_device_ids=true | all-gather | bytes 655360 | tf_op jit(solution)/shard_map/all_gather | solution.py:43
  273.4 0.9 bitcast_dynamic-update-slice_fusion.5
  274.3 0.9 bitcast_dynamic-update-slice_fusion.4
  275.2 0.9 bitcast_dynamic-update-slice_fusion.3
  276.1 0.9 bitcast_dynamic-update-slice_fusion.2
  277.0 0.9 bitcast_dynamic-update-slice_fusion.1
  277.9 0.9 bitcast_dynamic-update-slice_fusion
  278.8 4.9 all-to-all-done.3
  283.7 0.1 copy.46
  283.9 3.2 convolution_convert_fusion.2
  287.1 6.5 all_gather.19
  293.7 2.1 convert_reduce_fusion
  295.8 3.6 fusion.4
  299.5 1.0 copy.73
  300.5 11.0 %all-to-all-start.5 = ((bf16[64,48,128]{2,1,0:T(8,128)(2,1)}), bf16[64,48,128]{2,1,0:T(8,128)(2,1)S(1)}, u32[]{:S(2)}, u32[]{:S(2)}) async-start(bf16[64,48,128]{2,1,0:T(8,128)(2,1)} %bitcast.198), calls=%async_computation.5 | async-start | bytes 1572864 | tf_op jit(solution)/shard_map/all_to_all | solution.py:20
  311.5 1.2 fusion.30
  312.6 0.9 reshape.426
  313.5 23.8 %all-to-all-done.5 = bf16[64,48,128]{2,1,0:T(8,128)(2,1)S(1)} async-done(((bf16[64,48,128]{2,1,0:T(8,128)(2,1)}), bf16[64,48,128]{2,1,0:T(8,128)(2,1)S(1)}, u32[]{:S(2)}, u32[]{:S(2)}) %all-to-all-start.5) | async-done | bytes 786464 | tf_op jit(solution)/shard_map/all_to_all | solution.py:20
  337.3 5.8 all-to-all-start.4
  343.1 0.3 reshape.429
  343.4 0.4 copy.48
  343.8 1.2 fusion.28
  345.0 0.9 copy.50
  345.8 11.0 %all-to-all-done.4 = f32[64,2,512]{2,1,0:T(2,128)} async-done(((f32[64,2,512]{2,1,0:T(2,128)}), f32[64,2,512]{2,1,0:T(2,128)}, u32[]{:S(2)}, u32[]{:S(2)}) %all-to-all-start.4) | async-done | bytes 262176 | tf_op jit(solution)/shard_map/all_to_all | solution.py:20
  356.8 5.1 all-to-all-start.6
  361.9 176.7 %all-gather.3 = f32[64,1,512]{2,1,0:T(1,128)S(1)} all-gather(f32[1,1,512]{2,1,0:T(1,128)S(1)} %bitcast.214), channel_id=2, replica_groups=mesh['blk'=64,'rep'=4] {'blk'}, dimensions={0}, use_global_device_ids=true | all-gather | bytes 133120 | tf_op jit(solution)/shard_map/all_gather | solution.py:109
  538.6 0.7 reduce_sum.89
  539.3 1.7 fusion.12
  541.0 1.1 reduce_sum.87
  542.1 181.3 %all-gather.2 = f32[64,2,512]{2,1,0:T(2,128)S(1)} all-gather(f32[1,2,512]{2,1,0:T(2,128)S(1)} %bitcast.213), channel_id=1, replica_groups=mesh['blk'=64,'rep'=4] {'blk'}, dimensions={0}, use_global_device_ids=true | all-gather | bytes 266240 | tf_op jit(solution)/shard_map/all_gather | solution.py:112
  723.3 0.9 reshape.435
  724.2 0.7 fusion.11
  (33 shorter events, 0.6 us)
Async XLA Ops:
  0.6 211.6 %copy-start = (bf16[512,128]{1,0:T(8,128)(2,1)S(1)}, bf16[512,128]{1,0:T(8,128)(2,1)}, u32[]{:S(2)}) copy-start(bf16[512,128]{1,0:T(8,128)(2,1)} %param.9) | copy-start | bytes 393220
  2.6 210.9 %all-to-all-start = ((s32[64,1,16]{2,1,0:T(1,128)}), s32[64,1,16]{2,1,0:T(1,128)S(1)}, u32[]{:S(2)}, u32[]{:S(2)}) async-start(s32[64,1,16]{2,1,0:T(1,128)} %bitcast.70), calls=%async_computation | async-start | bytes 65536 | tf_op jit(solution)/shard_map/all_to_all | solution.py:20
  213.5 11.2 %copy-start.6 = (s32[64,1,16]{2,1,0:T(1,128)}, s32[64,1,16]{2,1,0:T(1,128)S(1)}, u32[]{:S(2)}) copy-start(s32[64,1,16]{2,1,0:T(1,128)S(1)} %all-to-all-done) | copy-start | bytes 12292
  213.5 24.4 %all-to-all-start.1 = ((bf16[64,16,128]{2,1,0:T(8,128)(2,1)}), bf16[64,16,128]{2,1,0:T(8,128)(2,1)}, u32[]{:S(2)}, u32[]{:S(2)}) async-start(bf16[64,16,128]{2,1,0:T(8,128)(2,1)} %bitcast.71), calls=%async_computation.1 | async-start | bytes 524288 | tf_op jit(solution)/shard_map/all_to_all | solution.py:20
  240.0 17.7 %all-to-all-start.2 = ((bf16[64,8,128]{2,1,0:T(8,128)(2,1)}), bf16[64,8,128]{2,1,0:T(8,128)(2,1)}, u32[]{:S(2)}, u32[]{:S(2)}) async-start(bf16[64,8,128]{2,1,0:T(8,128)(2,1)} %bitcast.212), calls=%async_computation.2 | async-start | bytes 262144 | tf_op jit(solution)/shard_map/all_to_all | solution.py:20
  260.2 23.6 %all-to-all-start.3 = ((bf16[64,48,128]{2,1,0:T(8,128)(2,1)}), bf16[64,48,128]{2,1,0:T(8,128)(2,1)S(1)}, u32[]{:S(2)}, u32[]{:S(2)}) async-start(bf16[64,48,128]{2,1,0:T(8,128)(2,1)} %reshape.423), calls=%async_computation.3 | async-start | bytes 1572864 | tf_op jit(solution)/shard_map/all_to_all | solution.py:20
  265.4 12.4 %copy-start.1 = (bf16[4,128,4,128]{3,2,1,0:T(4,128)(2,1)S(1)}, bf16[4,128,4,128]{3,2,1,0:T(4,128)(2,1)}, u32[]{:S(2)}) copy-start(bf16[4,128,4,128]{3,2,1,0:T(4,128)(2,1)} %select_select_fusion) | copy-start | bytes 1572868
  274.3 9.6 %copy-start.5 = (bf16[512,128]{1,0:T(8,128)(2,1)S(1)}, bf16[512,128]{1,0:T(8,128)(2,1)}, u32[]{:S(2)}) copy-start(bf16[512,128]{1,0:T(8,128)(2,1)} %fusion.3) | copy-start | bytes 393220
  283.7 9.9 %copy-start.4 = (bf16[512,512]{1,0:T(8,128)(2,1)S(1)}, bf16[512,512]{1,0:T(8,128)(2,1)}, u32[]{:S(2)}) copy-start(bf16[512,512]{1,0:T(8,128)(2,1)} %all_gather.20) | copy-start | bytes 1572868
  283.7 9.9 %copy-start.7 = (bf16[512,512]{1,0:T(8,128)(2,1)S(1)}, bf16[512,512]{1,0:T(8,128)(2,1)}, u32[]{:S(2)}) copy-start(bf16[512,512]{1,0:T(8,128)(2,1)} %param.17) | copy-start | bytes 1572868
  283.7 9.9 %copy-start.8 = (f32[512]{0:T(512)S(1)}, f32[512]{0:T(512)}, u32[]{:S(2)}) copy-start(f32[512]{0:T(512)} %param.16) | copy-start | bytes 6148
  287.1 8.7 %copy-start.3 = (bf16[512,128]{1,0:T(8,128)(2,1)}, bf16[512,128]{1,0:T(8,128)(2,1)S(1)}, u32[]{:S(2)}) copy-start(bf16[512,128]{1,0:T(8,128)(2,1)S(1)} %convolution_convert_fusion.2) | copy-start | bytes 393220
  293.7 2.1 copy-start.2
  300.5 36.8 %all-to-all-start.5 = ((bf16[64,48,128]{2,1,0:T(8,128)(2,1)}), bf16[64,48,128]{2,1,0:T(8,128)(2,1)S(1)}, u32[]{:S(2)}, u32[]{:S(2)}) async-start(bf16[64,48,128]{2,1,0:T(8,128)(2,1)} %bitcast.198), calls=%async_computation.5 | async-start | bytes 1572864 | tf_op jit(solution)/shard_map/all_to_all | solution.py:20
  337.3 19.5 %all-to-all-start.4 = ((f32[64,2,512]{2,1,0:T(2,128)}), f32[64,2,512]{2,1,0:T(2,128)}, u32[]{:S(2)}, u32[]{:S(2)}) async-start(f32[64,2,512]{2,1,0:T(2,128)} %reshape.426), calls=%async_computation.4 | async-start | bytes 524288 | tf_op jit(solution)/shard_map/all_to_all | solution.py:20
  356.8 367.4 %all-to-all-start.6 = ((f32[64,8,128]{2,1,0:T(8,128)}), f32[64,8,128]{2,1,0:T(8,128)S(1)}, u32[]{:S(2)}, u32[]{:S(2)}) async-start(f32[64,8,128]{2,1,0:T(8,128)} %copy.50), calls=%async_computation.6 | async-start | bytes 524288 | tf_op jit(solution)/shard_map/all_to_all | solution.py:20
where the time goes:
time: 726 us; the launch traced here: 725 us
  blocking collectives  547 us (75%)
  starting transfers between devices  58.2 us (8%)
  waiting for transfers between devices  57.9 us (8%)
  local copies, waits for them, and re-layouts  17.3 us (2%)
  matrix products  16.1 us (2%)
  between operations  14.3 us (2%)
  other arithmetic  13.6 us (2%)
    all_gather x1, blocking collectives, per_device(): lax.all_gather(jnp.sum(weight_part, axis=0), 'blk', axis=0, tiled=True)  181 us
    all_gather x1, blocking collectives, per_device(): bias_grad = jnp.sum(lax.all_gather(bias_part, 'blk', axis=0), axis=0)  177 us
    all_gather x1, blocking collectives, per_device(): lax.all_gather(tile_counts[0], 'blk', axis=0).reshape(blocks, blocks)  175 us
    all_to_all x7, starting transfers between devices, exchange(): return lax.all_to_all(x, 'blk', split_axis=0, concat_axis=0, tiled=True)  58.2 us
    all_to_all x7, waiting for transfers between devices, exchange(): return lax.all_to_all(x, 'blk', split_axis=0, concat_axis=0, tiled=True)  57.9 us
    dot_general x10, matrix products, dot(): return lax.dot_general(a, b, (dims, ((), ())), preferred_element_type=F32)  16.1 us
  transfers between devices with their start and end apart: 7, of which 5 were waited for; matrix products, arithmetic and copies ran while one was open for 4% of the time, Pallas kernels for 0%

commit v1 on v0

--- a/solution.py
+++ b/solution.py
@@ -109,7 +109,9 @@
     bias_grad = jnp.sum(lax.all_gather(bias_part, "blk", axis=0), axis=0)
     wide = weight_part.shape[1]
     weight_part = exchange(weight_part.reshape(blocks, -1, wide))
-    weight_grad = lax.all_gather(jnp.sum(weight_part, axis=0), "blk", axis=0, tiled=True)
+    block = jnp.sum(weight_part, axis=0)
+    outgoing = jnp.stack([block] * lax.axis_size("blk"))
+    weight_grad = jnp.concatenate(lax.all_to_all(outgoing, "blk", 0, 0), axis=0)
     return (output, weight_grad, bias_grad, feature_grad)
 
 

time: 726 us -> 566 us (0.78)
  blocking collectives: 547 us -> 366 us
  waiting for transfers between devices: 57.9 us -> 68.5 us
    all_gather x1 -> x0, blocking collectives: 181 us -> none  [per_device(): lax.all_gather(jnp.sum(weight_part, axis=0), 'blk', axis=0, tiled=True)]
    all_to_all x0 -> x1, waiting for transfers between devices: none -> 10.5 us  [per_device(): weight_grad = jnp.concatenate(lax.all_to_all(outgoing, 'blk', 0, 0), axis=0)]
  transfers between devices with their start and end apart: 7 -> 8, of which waited for: 5 -> 6; matrix products, arithmetic and copies ran while one was open for 4% -> 6% of each run, Pallas kernels for 0% -> 0%
where the time goes in v1:
time: 566 us; the launch traced here: 559 us
  blocking collectives  366 us (65%)
  waiting for transfers between devices  68.5 us (12%)
  starting transfers between devices  63.5 us (11%)
  local copies, waits for them, and re-layouts  19 us (3%)
  matrix products  15.2 us (3%)
  between operations  14.3 us (3%)
  other arithmetic  12.6 us (2%)
    all_gather x1, blocking collectives, per_device(): bias_grad = jnp.sum(lax.all_gather(bias_part, 'blk', axis=0), axis=0)  176 us
    all_gather x1, blocking collectives, per_device(): lax.all_gather(tile_counts[0], 'blk', axis=0).reshape(blocks, blocks)  175 us
    all_to_all x7, waiting for transfers between devices, exchange(): return lax.all_to_all(x, 'blk', split_axis=0, concat_axis=0, tiled=True)  58.1 us
    all_to_all x7, starting transfers between devices, exchange(): return lax.all_to_all(x, 'blk', split_axis=0, concat_axis=0, tiled=True)  57.6 us
    dot_general x10, matrix products, dot(): return lax.dot_general(a, b, (dims, ((), ())), preferred_element_type=F32)  15.2 us
  transfers between devices with their start and end apart: 8, of which 6 were waited for; matrix products, arithmetic and copies ran while one was open for 6% of the time, Pallas kernels for 0%

profile of v1, /device:TPU:32, one launch (start us, length us, event | category | flops | bytes accessed | tf_op | source)
XLA Modules:
  0.0 559.2 jit_solution(1920977353587183758)
XLA Ops:
  0.6 0.7 fusion.22
  1.4 0.2 fusion.5
  1.6 0.3 select_reduce_fusion
  1.9 0.7 sub.17
  2.6 14.2 %all-to-all-start = ((s32[64,1,16]{2,1,0:T(1,128)}), s32[64,1,16]{2,1,0:T(1,128)S(1)}, u32[]{:S(2)}, u32[]{:S(2)}) async-start(s32[64,1,16]{2,1,0:T(1,128)} %bitcast.70), calls=%async_computation | async-start | bytes 65536 | tf_op jit(solution)/shard_map/all_to_all | solution.py:20
  16.8 175.0 %all-gather.1 = s32[64,1,64]{2,1,0:T(1,128)S(1)} all-gather(s32[1,1,64]{2,1,0:T(1,128)} %bitcast.213), channel_id=1, replica_groups=mesh['blk'=64,'rep'=4] {'blk'}, dimensions={0}, use_global_device_ids=true | all-gather | bytes 16640 | tf_op jit(solution)/shard_map/all_gather | solution.py:44
  192.1 0.8 select_reduce_fusion.1
  192.9 0.7 fusion.27
  202.6 1.0 multiply_reduce_fusion.1
  203.8 0.6 slice_bitcast_fusion.3
  208.9 2.0 dynamic-slice_bitcast_fusion.3
  210.9 0.4 select_select_fusion.5
  211.4 0.4 select_select_fusion.6
  211.8 0.4 select_select_fusion.4
  212.3 1.2 fusion.2
  213.5 11.2 %all-to-all-start.1 = ((bf16[64,16,128]{2,1,0:T(8,128)(2,1)}), bf16[64,16,128]{2,1,0:T(8,128)(2,1)}, u32[]{:S(2)}, u32[]{:S(2)}) async-start(bf16[64,16,128]{2,1,0:T(8,128)(2,1)} %bitcast.71), calls=%async_computation.1 | async-start | bytes 524288 | tf_op jit(solution)/shard_map/all_to_all | solution.py:20
  224.6 0.4 select_select_fusion.3
  225.1 0.4 select_select_fusion.2
  225.5 1.3 select_select_fusion.1
  226.8 0.5 broadcast.247
  227.3 1.5 reduce.4
  228.9 9.0 %all-to-all-done.1 = bf16[64,16,128]{2,1,0:T(8,128)(2,1)} async-done(((bf16[64,16,128]{2,1,0:T(8,128)(2,1)}), bf16[64,16,128]{2,1,0:T(8,128)(2,1)}, u32[]{:S(2)}, u32[]{:S(2)}) %all-to-all-start.1) | async-done | bytes 262176 | tf_op jit(solution)/shard_map/all_to_all | solution.py:20
  237.9 2.1 fusion.3
  240.0 5.7 %all-to-all-start.2 = ((bf16[64,8,128]{2,1,0:T(8,128)(2,1)}), bf16[64,8,128]{2,1,0:T(8,128)(2,1)}, u32[]{:S(2)}, u32[]{:S(2)}) async-start(bf16[64,8,128]{2,1,0:T(8,128)(2,1)} %bitcast.211), calls=%async_computation.2 | async-start | bytes 262144 | tf_op jit(solution)/shard_map/all_to_all | solution.py:20
  245.7 1.2 select_select_fusion
  247.0 0.7 and.71
  247.6 0.9 bitcast_dynamic-update-slice_fusion.6
  248.5 9.1 %all-to-all-done.2 = bf16[64,8,128]{2,1,0:T(8,128)(2,1)} async-done(((bf16[64,8,128]{2,1,0:T(8,128)(2,1)}), bf16[64,8,128]{2,1,0:T(8,128)(2,1)}, u32[]{:S(2)}, u32[]{:S(2)}) %all-to-all-start.2) | async-done | bytes 131104 | tf_op jit(solution)/shard_map/all_to_all | solution.py:20
  257.7 1.3 convolution_convert_fusion
  259.0 1.2 reshape.428
  260.2 5.3 all-to-all-start.3
  265.4 8.0 %all_gather.17 = bf16[512,512]{1,0:T(8,128)(2,1)} all-gather(bf16[128,512]{1,0:T(8,128)(2,1)} %param.15), channel_id=1, replica_groups=mesh['blk'=64,'rep'=4] {'rep'}, dimensions={0}, use_global_device_ids=true | all-gather | bytes 655360 | tf_op jit(solution)/shard_map/all_gather | solution.py:43
  273.4 0.9 bitcast_dynamic-update-slice_fusion.5
  274.3 0.9 bitcast_dynamic-update-slice_fusion.4
  275.2 0.9 bitcast_dynamic-update-slice_fusion.3
  276.1 0.9 bitcast_dynamic-update-slice_fusion.2
  277.0 0.9 bitcast_dynamic-update-slice_fusion.1
  277.9 0.9 bitcast_dynamic-update-slice_fusion
  278.8 5.0 all-to-all-done.3
  283.7 0.1 copy.46
  283.9 3.2 convolution_convert_fusion.2
  287.1 6.5 %all_gather.16 = bf16[512,512]{1,0:T(8,128)(2,1)S(1)} all-gather(bf16[512,128]{1,0:T(8,128)(2,1)S(1)} %convolution_convert_fusion.2), channel_id=1, replica_groups=mesh['blk'=64,'rep'=4] {'rep'}, dimensions={1}, use_global_device_ids=true | all-gather | bytes 655360 | tf_op jit(solution)/shard_map/all_gather | solution.py:92
  293.7 2.1 convert_reduce_fusion
  295.8 0.2 fusion.30
  296.0 0.9 reshape.431
  296.9 11.0 %all-to-all-start.4 = ((f32[64,2,512]{2,1,0:T(2,128)}), f32[64,2,512]{2,1,0:T(2,128)S(1)}, u32[]{:S(2)}, u32[]{:S(2)}) async-start(f32[64,2,512]{2,1,0:T(2,128)} %reshape.431), calls=%async_computation.4 | async-start | bytes 524288 | tf_op jit(solution)/shard_map/all_to_all | solution.py:20
  307.9 3.6 fusion.4
  311.5 1.0 copy.73
  312.6 10.3 %all-to-all-done.4 = f32[64,2,512]{2,1,0:T(2,128)S(1)} async-done(((f32[64,2,512]{2,1,0:T(2,128)}), f32[64,2,512]{2,1,0:T(2,128)S(1)}, u32[]{:S(2)}, u32[]{:S(2)}) %all-to-all-start.4) | async-done | bytes 262176 | tf_op jit(solution)/shard_map/all_to_all | solution.py:20
  322.9 5.1 all-to-all-start.6
  328.1 24.7 %all-to-all-done.6 = bf16[64,48,128]{2,1,0:T(8,128)(2,1)S(1)} async-done(((bf16[64,48,128]{2,1,0:T(8,128)(2,1)}), bf16[64,48,128]{2,1,0:T(8,128)(2,1)S(1)}, u32[]{:S(2)}, u32[]{:S(2)}) %all-to-all-start.6) | async-done | bytes 786464 | tf_op jit(solution)/shard_map/all_to_all | solution.py:20
  352.8 0.8 stack.2
  353.6 5.9 %all-to-all-start.5 = ((f32[64,2,512]{2,1,0:T(2,128)}), f32[64,2,512]{2,1,0:T(2,128)}, u32[]{:S(2)}, u32[]{:S(2)}) async-start(f32[64,2,512]{2,1,0:T(2,128)} %stack.2), calls=%async_computation.5 | async-start | bytes 524288 | tf_op jit(solution)/shard_map/all_to_all | solution.py:114
  359.4 0.3 reshape.435
  359.8 0.4 copy.48
  360.1 1.2 fusion.28
  361.3 0.9 copy.50
  362.2 10.5 %all-to-all-done.5 = f32[64,2,512]{2,1,0:T(2,128)} async-done(((f32[64,2,512]{2,1,0:T(2,128)}), f32[64,2,512]{2,1,0:T(2,128)}, u32[]{:S(2)}, u32[]{:S(2)}) %all-to-all-start.5) | async-done | bytes 262176 | tf_op jit(solution)/shard_map/all_to_all | solution.py:114
  372.7 5.1 all-to-all-start.7
  377.8 176.5 %all-gather.2 = f32[64,1,512]{2,1,0:T(1,128)S(1)} all-gather(f32[1,1,512]{2,1,0:T(1,128)S(1)} %bitcast.212), channel_id=2, replica_groups=mesh['blk'=64,'rep'=4] {'blk'}, dimensions={0}, use_global_device_ids=true | all-gather | bytes 133120 | tf_op jit(solution)/shard_map/all_gather | solution.py:109
  554.3 0.7 reduce_sum.89
  555.0 1.7 fusion.12
  556.7 1.8 reshape.432
  558.5 0.7 fusion.11
  (31 shorter events, 0.8 us)
Async XLA Ops:
  0.6 211.6 %copy-start = (bf16[512,128]{1,0:T(8,128)(2,1)S(1)}, bf16[512,128]{1,0:T(8,128)(2,1)}, u32[]{:S(2)}) copy-start(bf16[512,128]{1,0:T(8,128)(2,1)} %param.9) | copy-start | bytes 393220
  2.6 210.9 %all-to-all-start = ((s32[64,1,16]{2,1,0:T(1,128)}), s32[64,1,16]{2,1,0:T(1,128)S(1)}, u32[]{:S(2)}, u32[]{:S(2)}) async-start(s32[64,1,16]{2,1,0:T(1,128)} %bitcast.70), calls=%async_computation | async-start | bytes 65536 | tf_op jit(solution)/shard_map/all_to_all | solution.py:20
  213.5 11.2 %copy-start.4 = (s32[64,1,16]{2,1,0:T(1,128)}, s32[64,1,16]{2,1,0:T(1,128)S(1)}, u32[]{:S(2)}) copy-start(s32[64,1,16]{2,1,0:T(1,128)S(1)} %all-to-all-done) | copy-start | bytes 12292
  213.5 24.4 %all-to-all-start.1 = ((bf16[64,16,128]{2,1,0:T(8,128)(2,1)}), bf16[64,16,128]{2,1,0:T(8,128)(2,1)}, u32[]{:S(2)}, u32[]{:S(2)}) async-start(bf16[64,16,128]{2,1,0:T(8,128)(2,1)} %bitcast.71), calls=%async_computation.1 | async-start | bytes 524288 | tf_op jit(solution)/shard_map/all_to_all | solution.py:20
  240.0 17.7 %all-to-all-start.2 = ((bf16[64,8,128]{2,1,0:T(8,128)(2,1)}), bf16[64,8,128]{2,1,0:T(8,128)(2,1)}, u32[]{:S(2)}, u32[]{:S(2)}) async-start(bf16[64,8,128]{2,1,0:T(8,128)(2,1)} %bitcast.211), calls=%async_computation.2 | async-start | bytes 262144 | tf_op jit(solution)/shard_map/all_to_all | solution.py:20
  260.2 23.6 %all-to-all-start.3 = ((bf16[64,48,128]{2,1,0:T(8,128)(2,1)}), bf16[64,48,128]{2,1,0:T(8,128)(2,1)S(1)}, u32[]{:S(2)}, u32[]{:S(2)}) async-start(bf16[64,48,128]{2,1,0:T(8,128)(2,1)} %reshape.428), calls=%async_computation.3 | async-start | bytes 1572864 | tf_op jit(solution)/shard_map/all_to_all | solution.py:20
  265.4 12.4 %copy-start.1 = (bf16[4,128,4,128]{3,2,1,0:T(4,128)(2,1)S(1)}, bf16[4,128,4,128]{3,2,1,0:T(4,128)(2,1)}, u32[]{:S(2)}) copy-start(bf16[4,128,4,128]{3,2,1,0:T(4,128)(2,1)} %select_select_fusion) | copy-start | bytes 1572868
  283.7 9.9 %copy-start.3 = (bf16[512,512]{1,0:T(8,128)(2,1)S(1)}, bf16[512,512]{1,0:T(8,128)(2,1)}, u32[]{:S(2)}) copy-start(bf16[512,512]{1,0:T(8,128)(2,1)} %all_gather.17) | copy-start | bytes 1572868
  283.7 9.9 %copy-start.5 = (bf16[512,512]{1,0:T(8,128)(2,1)S(1)}, bf16[512,512]{1,0:T(8,128)(2,1)}, u32[]{:S(2)}) copy-start(bf16[512,512]{1,0:T(8,128)(2,1)} %param.17) | copy-start | bytes 1572868
  283.7 9.9 %copy-start.6 = (f32[512]{0:T(512)S(1)}, f32[512]{0:T(512)}, u32[]{:S(2)}) copy-start(f32[512]{0:T(512)} %param.16) | copy-start | bytes 6148
  293.7 14.2 %copy-start.2 = (bf16[128,512]{1,0:T(8,128)(2,1)S(1)}, bf16[128,512]{1,0:T(8,128)(2,1)}, u32[]{:S(2)}) copy-start(bf16[128,512]{1,0:T(8,128)(2,1)} %param.15) | copy-start | bytes 393220
  296.9 26.0 %all-to-all-start.4 = ((f32[64,2,512]{2,1,0:T(2,128)}), f32[64,2,512]{2,1,0:T(2,128)S(1)}, u32[]{:S(2)}, u32[]{:S(2)}) async-start(f32[64,2,512]{2,1,0:T(2,128)} %reshape.431), calls=%async_computation.4 | async-start | bytes 524288 | tf_op jit(solution)/shard_map/all_to_all | solution.py:20
  322.9 29.9 %all-to-all-start.6 = ((bf16[64,48,128]{2,1,0:T(8,128)(2,1)}), bf16[64,48,128]{2,1,0:T(8,128)(2,1)S(1)}, u32[]{:S(2)}, u32[]{:S(2)}) async-start(bf16[64,48,128]{2,1,0:T(8,128)(2,1)} %bitcast.197), calls=%async_computation.6 | async-start | bytes 1572864 | tf_op jit(solution)/shard_map/all_to_all | solution.py:20
  353.6 19.1 %all-to-all-start.5 = ((f32[64,2,512]{2,1,0:T(2,128)}), f32[64,2,512]{2,1,0:T(2,128)}, u32[]{:S(2)}, u32[]{:S(2)}) async-start(f32[64,2,512]{2,1,0:T(2,128)} %stack.2), calls=%async_computation.5 | async-start | bytes 524288 | tf_op jit(solution)/shard_map/all_to_all | solution.py:114
  372.7 185.9 %all-to-all-start.7 = ((f32[64,8,128]{2,1,0:T(8,128)}), f32[64,8,128]{2,1,0:T(8,128)S(1)}, u32[]{:S(2)}, u32[]{:S(2)}) async-start(f32[64,8,128]{2,1,0:T(8,128)} %copy.50), calls=%async_computation.7 | async-start | bytes 524288 | tf_op jit(solution)/shard_map/all_to_all | solution.py:20
